TPU v7x, 32 devices: a whole 2x2x4 slice. The times are simulated.
32 devices in a mesh: freq: 8 (over z, x), depth: 4 (over y, core).
Axes of the slice: x: 2, y: 2, z: 4, core: 2. Of those that a mesh axis runs over, the one named last changes fastest.
Arguments:
- slowness: float32 [4, 24576], P('depth', 'freq'), may hold values from 0.25 to 1
- freq_index: int32 [16], P('freq'), may hold values from 0 to 15, each once
- taps: float32 [16, 2, 11], replicated, may hold values from -1 to 1, as said below
- source_top: float32 [16, 4, 2, 24, 1024], P('freq', 'depth'), may hold values from -6 to 6
- adjoint_source: float32 [16, 4, 2, 24, 1024], P('freq', 'depth'), may hold values from -6 to 6
Outputs:
- gradient: float32 [4, 24576], P('depth', 'freq')
Inputs may be any that keep to these rules, and one draw needn't show every extreme that they name: `freq_index`: each of 0 to 15 appears once. In each frequency the absolute values of the complex taps sum to at most 1.
All inputs are finite; a program needn't handle non-finite values.
Results may differ from a plain program's by a relative error of at most 0.0003.
Values sent between devices are 32-bit elements; how exact they have to be, the bound alone decides.
A program may use at most 64 MiB of HBM per device.

v0:
```python
import jax
import jax.numpy as jnp
from jax import lax
from jax.sharding import PartitionSpec as P


def from_behind(value, axis, steps):
    count = lax.axis_size(axis)
    leading, last = (max(0, -steps), min(count, count - steps))
    return lax.ppermute(value, axis, [(source, source + steps) for source in range(leading, last)])


def convolve(field_re, field_im, tap_re, tap_im, along, adjoint):
    along = field_re.ndim + along
    reach = tap_re.shape[-1] // 2
    extent = field_re.shape[along]
    widths = [(0, 0)] * field_re.ndim
    widths[along] = (reach, reach)
    padded_re = jnp.pad(field_re, widths)
    padded_im = jnp.pad(field_im, widths)
    out_re = jnp.zeros_like(field_re)
    out_im = jnp.zeros_like(field_im)
    for offset in range(2 * reach + 1):
        anchor = 2 * reach - offset if adjoint else offset
        shifted_re = lax.slice_in_dim(padded_re, anchor, anchor + extent, axis=along)
        shifted_im = lax.slice_in_dim(padded_im, anchor, anchor + extent, axis=along)
        coef_re = tap_re[..., offset][..., None, None]
        coef_im = tap_im[..., offset][..., None, None]
        if adjoint:
            out_re = out_re + coef_re * shifted_re + coef_im * shifted_im
            out_im = out_im + coef_re * shifted_im - coef_im * shifted_re
        else:
            out_re = out_re + coef_re * shifted_re - coef_im * shifted_im
            out_im = out_im + coef_re * shifted_im + coef_im * shifted_re
    return (out_re, out_im)


def forward_step(field_re, field_im, tap_re, tap_im, phase_cos, phase_sin):
    mid_re, mid_im = convolve(field_re, field_im, tap_re, tap_im, -1, False)
    mid_re, mid_im = convolve(mid_re, mid_im, tap_re, tap_im, -2, False)
    return (phase_cos * mid_re - phase_sin * mid_im, phase_sin * mid_re + phase_cos * mid_im)


def adjoint_step(field_re, field_im, tap_re, tap_im, phase_cos, phase_sin):
    mid_re = phase_cos * field_re + phase_sin * field_im
    mid_im = phase_cos * field_im - phase_sin * field_re
    mid_re, mid_im = convolve(mid_re, mid_im, tap_re, tap_im, -2, True)
    return convolve(mid_re, mid_im, tap_re, tap_im, -1, True)


def sweep(
    incoming, adj_re, adj_im, wave_re, wave_im, phase_cos, phase_sin, tap_re, tap_im, angular
):
    steps = adj_re.shape[1]
    carry = (incoming[:, 0], incoming[:, 1])
    terms = [None] * steps
    for step in reversed(range(steps)):
        mu_re = adj_re[:, step] + carry[0]
        mu_im = adj_im[:, step] + carry[1]
        terms[step] = jnp.sum(
            angular[:, None, None] * (mu_im * wave_re[:, step] - mu_re * wave_im[:, step]), axis=0
        )
        carry = adjoint_step(mu_re, mu_im, tap_re, tap_im, phase_cos[:, step], phase_sin[:, step])
    return (jnp.stack(carry, axis=1), jnp.stack(terms))


def on_device(slowness, freq_index, taps, source_top, adjoint_source):
    steps = slowness.shape[0]
    lines, cells = (source_top.shape[3], source_top.shape[4])
    whole = lax.all_gather(slowness, "freq", axis=1, tiled=True).reshape(steps, lines, cells)
    count = taps.shape[0]
    lanes = freq_index.shape[0]
    onehot = (freq_index[:, None] == jnp.arange(count, dtype=jnp.int32)[None, :]).astype(
        jnp.float32
    )
    tap_table = jnp.dot(
        onehot,
        taps.reshape(count, -1),
        precision=lax.Precision.HIGHEST,
        preferred_element_type=jnp.float32,
    ).reshape(lanes, 2, -1)
    tap_re, tap_im = (tap_table[:, 0], tap_table[:, 1])
    angular = 8.0 * (freq_index.astype(jnp.float32) + 1.0) / count
    phase = angular[:, None, None, None] * whole[None]
    phase_cos = jnp.cos(phase)
    phase_sin = jnp.sin(phase)
    field_re, field_im = (source_top[:, 0, 0], source_top[:, 0, 1])
    waves_re, waves_im = ([], [])
    field_re, field_im = forward_step(
        field_re, field_im, tap_re, tap_im, phase_cos[:, 0], phase_sin[:, 0]
    )
    waves_re.append(field_re)
    waves_im.append(field_im)
    wave_re = jnp.stack(waves_re, axis=1)
    wave_im = jnp.stack(waves_im, axis=1)
    adj_re = adjoint_source[:, :, 0]
    adj_im = adjoint_source[:, :, 1]
    depth_count = lax.axis_size("depth")

    def segment(turn, received):
        top, _ = sweep(
            received,
            adj_re,
            adj_im,
            wave_re,
            wave_im,
            phase_cos,
            phase_sin,
            tap_re,
            tap_im,
            angular,
        )
        return from_behind(top, "depth", -1)

    received = lax.fori_loop(
        0, depth_count - 1, segment, jnp.zeros((lanes, 2, lines, cells), jnp.float32)
    )
    _, image = sweep(
        received, adj_re, adj_im, wave_re, wave_im, phase_cos, phase_sin, tap_re, tap_im, angular
    )
    summed = lax.psum_scatter(
        image.reshape(steps, lines * cells), "freq", scatter_dimension=1, tiled=True
    )
    return summed / count


def solution(mesh):
    in_specs = (
        P("depth", "freq"),
        P("freq"),
        P(),
        P("freq", "depth", None, None, None),
        P("freq", "depth", None, None, None),
    )
    out_specs = P("depth", "freq")
    return jax.shard_map(
        on_device, mesh=mesh, in_specs=in_specs, out_specs=out_specs, check_vma=False
    )
```

profile of v0, /device:TPU:0, one launch (start us, length us, event | category | flops | bytes accessed | tf_op | source)
XLA Modules:
  0.0 324.1 jit_solution(15409046193173030078)
XLA Ops:
  6.5 0.7 add_multiply_fusion
  7.2 0.8 copy.21
  8.2 0.8 fusion.23
  9.9 1.1 slice_bitcast_fusion.23
  10.9 1.1 multiply_subtract_fusion.1
  12.1 1.1 multiply_add_fusion.1
  13.2 32.5 %all_gather.3 = f32[1,24576]{1,0:T(1,128)S(1)} all-gather(f32[1,3072]{1,0:T(1,128)} %param.7), channel_id=1, replica_groups=mesh['freq'=8,'depth'=4] {'freq'}, dimensions={1}, use_global_device_ids=true | all-gather | bytes 110592 | tf_op jit(solution)/shard_map/all_gather | solution.py:70
  46.3 0.9 reduce.47
  47.3 1.1 slice_bitcast_fusion.25
  48.4 34.6 %while.14 = (s32[]{:T(128)}, f32[2,2,24,1024]{3,2,0,1:T(8,128)S(1)}, f32[2,11]{0,1:T(8,128)S(1)}, f32[2,1,1,24,1024]{4,3,0,2,1:T(8,128)S(1)}, f32[2,1,1,24,1024]...) while((s32[]{:T(128)}, ...), condition=%wide.region_1.2_spmd.clone.clone, body=%wide.region_0.1_spmd.clone.clone.sunk | while | flops 8994818 | bytes 5997741 | solution.py:115
  48.4 0.8 fusion.30
  49.3 0.6 multiply_subtract_fusion.3
  50.6 1.1 add_bitcast_fusion.2
  51.7 1.1 subtract_bitcast_fusion.2
  52.9 1.3 collective-permute-start
  54.2 2.3 collective-permute-done
  56.5 0.8 fusion.30
  57.3 0.6 multiply_subtract_fusion.3
  58.6 1.1 add_bitcast_fusion.2
  59.7 1.1 subtract_bitcast_fusion.2
  60.9 1.3 collective-permute-start
  62.2 7.2 %collective-permute-done = f32[2,2,24,1024]{3,2,0,1:T(8,128)S(1)} collective-permute-done((f32[2,2,24,1024]{3,2,0,1:T(8,128)S(1)}, f32[2,2,24,1024]{3,2,0,1:T(8,128)S(1)}, u32[]{:S(2)}, u32[]{:S(2)}) %collective-permute-start) | collective-permute-done | bytes 393248 | tf_op jit(solution)/shard_map/while/body/eval_jaxpr/ppermute | solution.py:10
  69.4 0.8 fusion.30
  71.5 1.1 add_bitcast_fusion.2
  72.7 1.1 subtract_bitcast_fusion.2
  73.9 1.3 collective-permute-start
  75.2 7.8 %collective-permute-done = f32[2,2,24,1024]{3,2,0,1:T(8,128)S(1)} collective-permute-done((f32[2,2,24,1024]{3,2,0,1:T(8,128)S(1)}, f32[2,2,24,1024]{3,2,0,1:T(8,128)S(1)}, u32[]{:S(2)}, u32[]{:S(2)}) %collective-permute-start) | collective-permute-done | bytes 393248 | tf_op jit(solution)/shard_map/while/body/eval_jaxpr/ppermute | solution.py:10
  83.0 1.9 fusion.20
  84.9 6.8 %copy.35 = f32[1,24576]{0,1:T(8,128)} copy(f32[1,24576]{1,0:T(1,128)S(1)} %bitcast.158) | data formatting | bytes 196608
  91.7 10.0 %bitcast_bitcast_fusion = f32[24576,1]{1,0:T(8,128)} fusion(f32[1,24576]{0,1:T(8,128)} %copy.35), kind=kLoop, calls=%fused_computation.81 | loop fusion | bytes 196608
  101.7 213.0 %reduce-scatter.4.cloned.1.call-done = f32[3072,1]{1,0:T(8,128)} async-done(((f32[24576,1]{1,0:T(8,128)}), f32[3072,1]{1,0:T(8,128)}) %reduce-scatter.4.cloned.1.call-update) | async-done | bytes 12304
  314.8 1.9 copy.29
  (29 shorter events, 5.1 us)
Async XLA Ops:
  6.5 308.2 %reduce-scatter.4.cloned.1.call-start = ((), (), s32[]{:S(2)}) async-start(), calls=%async_computation.1 | async-start | bytes 14155776
  12.1 70.9 %copy-start = (f32[2,1,2,24,1024]{4,3,2,1,0:T(8,128)S(1)}, f32[2,1,2,24,1024]{4,3,2,1,0:T(8,128)}, u32[]{:S(2)}) copy-start(f32[2,1,2,24,1024]{4,3,2,1,0:T(8,128)} %param.11) | copy-start | bytes 1179652
  52.9 3.6 %collective-permute-start = (f32[2,2,24,1024]{3,2,0,1:T(8,128)S(1)}, f32[2,2,24,1024]{3,2,0,1:T(8,128)S(1)}, u32[]{:S(2)}, u32[]{:S(2)}) collective-permute-start(f32[2,2,24,1024]{3,2,0,1:T(8,128)S(1)} %pad_maximum_fusion.2), channel_id=1, source_target_pairs={{1,0},{2,1},{3,2},{5,4},{6,5},{7,6},{9,8},{10,9},{11,10},{13,12},{... | collective-permute-start | bytes 1179656 | tf_op jit(solution)/shard_map/while/body/eval_jaxpr/ppermute | solution.py:10
  60.9 8.5 %collective-permute-start = (f32[2,2,24,1024]{3,2,0,1:T(8,128)S(1)}, f32[2,2,24,1024]{3,2,0,1:T(8,128)S(1)}, u32[]{:S(2)}, u32[]{:S(2)}) collective-permute-start(f32[2,2,24,1024]{3,2,0,1:T(8,128)S(1)} %pad_maximum_fusion.2), channel_id=1, source_target_pairs={{1,0},{2,1},{3,2},{5,4},{6,5},{7,6},{9,8},{10,9},{11,10},{13,12},{... | collective-permute-start | bytes 1179656 | tf_op jit(solution)/shard_map/while/body/eval_jaxpr/ppermute | solution.py:10
  73.9 9.1 %collective-permute-start = (f32[2,2,24,1024]{3,2,0,1:T(8,128)S(1)}, f32[2,2,24,1024]{3,2,0,1:T(8,128)S(1)}, u32[]{:S(2)}, u32[]{:S(2)}) collective-permute-start(f32[2,2,24,1024]{3,2,0,1:T(8,128)S(1)} %pad_maximum_fusion.2), channel_id=1, source_target_pairs={{1,0},{2,1},{3,2},{5,4},{6,5},{7,6},{9,8},{10,9},{11,10},{13,12},{... | collective-permute-start | bytes 1179656 | tf_op jit(solution)/shard_map/while/body/eval_jaxpr/ppermute | solution.py:10
Sparse Core Ops, SparseCore 0:
  101.9 212.8 reduce-scatter.3
where the time goes:
time: 324 us
  waiting for transfers between devices  230 us (71%)
  blocking collectives  32.5 us (10%)
  local copies, waits for them, and re-layouts  23.4 us (7%)
  other arithmetic  19.5 us (6%)
  between operations  13.5 us (4%)
  starting transfers between devices  3.88 us (1%)
    unnamed x2, waiting for transfers between devices  213 us
    all_gather x1, blocking collectives, on_device(): lax.all_gather(slowness, 'freq', axis=1, tiled=True)  32.5 us
    unnamed x10, local copies, waits for them, and re-layouts  20.8 us
    ppermute x3, waiting for transfers between devices, from_behind(): lax.ppermute(value, axis, [(source, source + steps) for source in range(l...  17.3 us
    another operation x9, other arithmetic, sweep(): return (jnp.stack(carry, axis=1), jnp.stack(terms))  6.86 us
  transfers between devices with their start and end apart: 4, of which 4 were waited for; matrix products, arithmetic and copies ran while one was open for 0% of the time, Pallas kernels for 0%

commit v1 on v0

v1 whole, which is shorter than its diff:
```python
import functools
import math

import jax
import jax.numpy as jnp
from jax import lax
from jax.experimental import pallas as pl
from jax.experimental.pallas import tpu as pltpu
from jax.sharding import PartitionSpec as P

MESH = pl.DeviceIdType.MESH
LANES = 128
SUB = 8
BLOCK = 4
CHUNK = 8

PI_HIGH = 3.140625
PI_LOW = math.pi - PI_HIGH


def sin_cos(phase):
    turns = jnp.floor(phase * (1.0 / math.pi) + 0.5)
    rest = (phase - turns * PI_HIGH) - turns * PI_LOW
    sign = 1.0 - 2.0 * (turns - 2.0 * jnp.floor(turns * 0.5))
    square = rest * rest
    odd = -1.0 / math.factorial(11)
    for n, s in ((9, 1), (7, -1), (5, 1), (3, -1), (1, 1)):
        odd = odd * square + s / math.factorial(n)
    even = 1.0 / math.factorial(12)
    for n, s in ((10, -1), (8, 1), (6, -1), (4, 1), (2, -1), (0, 1)):
        even = even * square + s / math.factorial(n)
    return sign * rest * odd, sign * even


def shifted(value, reach):
    lane = lax.broadcasted_iota(jnp.int32, value.shape, 2)
    row = lax.broadcasted_iota(jnp.int32, value.shape, 1)
    after = jnp.where(row < SUB - 1, pltpu.roll(value, SUB - 1, 1), 0.0)
    before = jnp.where(row > 0, pltpu.roll(value, 1, 1), 0.0)
    out = {0: value}
    for o in range(1, reach + 1):
        out[o] = pltpu.roll(jnp.where(lane >= o, value, after), LANES - o, 2)
        out[-o] = pltpu.roll(jnp.where(lane < LANES - o, value, before), o, 2)
    return out


def filtered(at_re, at_im, taps, adjoint):
    reach = len(taps) // 2
    out_re = out_im = None
    for k, (t_re, t_im) in enumerate(taps):
        o = reach - k if adjoint else k - reach
        u_re, u_im = at_re(o), at_im(o)
        if adjoint:
            t_im = -t_im
        add_re = t_re * u_re - t_im * u_im
        add_im = t_re * u_im + t_im * u_re
        out_re = add_re if out_re is None else out_re + add_re
        out_im = add_im if out_im is None else out_im + add_im
    return out_re, out_im


def filter_x(re, im, taps, adjoint):
    reach = len(taps) // 2
    all_re, all_im = shifted(re, reach), shifted(im, reach)
    return filtered(lambda o: all_re[o], lambda o: all_im[o], taps, adjoint)


def kernel(
    peers, depths, lanes, lines, reach, count, per_piece, whole_lines,
    slow_ref, index_ref, taps_ref, source_ref, adjoint_ref, out_ref,
    source_in, adjoint_in, wave, adj, padded, slow, cosine, sine,
    arrived, leaving, grad, gathered,
    in_sem, slow_send, slow_recv, mu_send, mu_recv, grad_send, grad_recv,
):
    me = lax.axis_index("freq")
    d = lax.axis_index("depth")
    chunks = lines // CHUNK

    load_source = pltpu.make_async_copy(source_ref, source_in, in_sem.at[0])
    load_adjoint = pltpu.make_async_copy(adjoint_ref, adjoint_in, in_sem.at[1])
    load_source.start()
    load_adjoint.start()

    barrier = pltpu.get_barrier_semaphore()

    def peer(i):
        return lax.rem(me + i, peers)

    def greet(i, carry):
        pl.semaphore_signal(barrier, inc=1, device_id={"freq": peer(i)}, device_id_type=MESH)
        return carry

    lax.fori_loop(1, peers, greet, 0)

    @pl.when(d < depths - 1)
    def _():
        pl.semaphore_signal(barrier, inc=1, device_id={"depth": d + 1}, device_id_type=MESH)

    def piece(i):
        return pl.ds(i * per_piece, per_piece)

    slow[piece(me)] = slow_ref[...]
    margin = jnp.zeros((reach, SUB, LANES), jnp.float32)
    for part in range(2):
        padded[part, pl.ds(0, reach)] = margin
        padded[part, pl.ds(lines + reach, reach)] = margin
    grad[...] = jnp.zeros_like(grad)

    @pl.when(d == depths - 1)
    def _():
        arrived[...] = jnp.zeros_like(arrived)

    pl.semaphore_wait(barrier, jnp.where(d > 0, peers, peers - 1))

    def send_slow(i):
        return pltpu.make_async_remote_copy(
            src_ref=slow_ref, dst_ref=slow.at[piece(me)],
            send_sem=slow_send.at[peer(i)], recv_sem=slow_recv.at[me],
            device_id={"freq": peer(i)}, device_id_type=MESH,
        )

    def recv_slow(i):
        return pltpu.make_async_remote_copy(
            src_ref=slow_ref, dst_ref=slow.at[piece(peer(i))],
            send_sem=slow_send.at[peer(i)], recv_sem=slow_recv.at[peer(i)],
            device_id={"freq": peer(i)}, device_id_type=MESH,
        )

    def start_slow(i, carry):
        send_slow(i).start()
        return carry

    lax.fori_loop(1, peers, start_slow, 0)

    def tap_list(f):
        row = index_ref[f]
        return [(taps_ref[k, 0, row], taps_ref[k, 1, row]) for k in range(2 * reach + 1)]

    def angular(f):
        return 8.0 * (index_ref[f].astype(jnp.float32) + 1.0) / count

    def blocks(y, n=BLOCK):
        return pl.ds(y, n)

    def unfold(from_ref, to_ref):
        def body(i, carry):
            f, part = i // 2, i % 2
            for t in range(lines // SUB):
                rows = from_ref[f, part, pl.ds(t * SUB, SUB), :]
                to_ref[f, part, pl.ds(t * SUB, SUB)] = rows.reshape(SUB, SUB, LANES)
            return carry

        lax.fori_loop(0, 2 * lanes, body, 0)

    def filter_y(y, taps, adjoint):
        return filtered(
            lambda o: padded[0, blocks(y + reach + o)],
            lambda o: padded[1, blocks(y + reach + o)],
            taps, adjoint,
        )

    load_source.wait()
    unfold(source_in, wave)

    def forward(f, carry):
        taps = tap_list(f)

        def along_x(b, c):
            y = b * BLOCK
            re, im = filter_x(wave[f, 0, blocks(y)], wave[f, 1, blocks(y)], taps, False)
            padded[0, blocks(y + reach)] = re
            padded[1, blocks(y + reach)] = im
            return c

        def along_y(b, c):
            y = b * BLOCK
            re, im = filter_y(y, taps, False)
            wave[f, 0, blocks(y)] = re
            wave[f, 1, blocks(y)] = im
            return c

        lax.fori_loop(0, lines // BLOCK, along_x, 0)
        lax.fori_loop(0, lines // BLOCK, along_y, 0)
        return carry

    lax.fori_loop(0, lanes, forward, 0)

    load_adjoint.wait()
    unfold(adjoint_in, adj)

    def wait_slow(i, carry):
        recv_slow(i).wait_recv()
        return carry

    lax.fori_loop(1, peers, wait_slow, 0)

    def slow_block(y):
        if whole_lines:
            return slow[blocks(y)]
        per_line = SUB * peers // (lines * SUB)
        return slow[pl.ds(y * per_line, BLOCK * per_line)].reshape(BLOCK, SUB, LANES)

    def phases(f, carry):
        w = angular(f)

        def body(b, c):
            y = b * BLOCK
            s, co = sin_cos(w * slow_block(y))
            sine[f, blocks(y)] = s
            cosine[f, blocks(y)] = co
            re, im = wave[f, 0, blocks(y)], wave[f, 1, blocks(y)]
            wave[f, 0, blocks(y)] = w * (co * re - s * im)
            wave[f, 1, blocks(y)] = w * (s * re + co * im)
            return c

        lax.fori_loop(0, lines // BLOCK, body, 0)
        return carry

    lax.fori_loop(0, lanes, phases, 0)

    def hop(f, chunk):
        rows = pl.ds(chunk * CHUNK, CHUNK)
        slot = f * chunks + chunk
        return pltpu.make_async_remote_copy(
            src_ref=leaving.at[f, rows], dst_ref=arrived.at[f, rows],
            send_sem=mu_send.at[slot], recv_sem=mu_recv.at[slot],
            device_id={"depth": lax.max(d - 1, 0)}, device_id_type=MESH,
        )

    def add_grad(y, term):
        if whole_lines:
            grad[blocks(y)] += term
        else:
            per_line = SUB * peers // (lines * SUB)
            grad[pl.ds(y * per_line, BLOCK * per_line)] += term.reshape(
                BLOCK * per_line, SUB // per_line, LANES
            )

    def chain(f, carry):
        taps = tap_list(f)

        def take(chunk):
            @pl.when(d < depths - 1)
            def _():
                hop(f, chunk).wait_recv()

            def body(b, c):
                y = chunk * CHUNK + b * BLOCK
                mu_re = adj[f, 0, blocks(y)] + arrived[f, blocks(y), 0]
                mu_im = adj[f, 1, blocks(y)] + arrived[f, blocks(y), 1]
                add_grad(y, mu_im * wave[f, 0, blocks(y)] - mu_re * wave[f, 1, blocks(y)])
                co, s = cosine[f, blocks(y)], sine[f, blocks(y)]
                padded[0, blocks(y + reach)] = co * mu_re + s * mu_im
                padded[1, blocks(y + reach)] = co * mu_im - s * mu_re
                return c

            lax.fori_loop(0, CHUNK // BLOCK, body, 0)

        def give(chunk):
            @pl.when(d > 0)
            def _():
                def body(b, c):
                    y = chunk * CHUNK + b * BLOCK
                    re, im = filter_y(y, taps, True)
                    re, im = filter_x(re, im, taps, True)
                    leaving[f, blocks(y), 0] = re
                    leaving[f, blocks(y), 1] = im
                    return c

                lax.fori_loop(0, CHUNK // BLOCK, body, 0)
                hop(f, chunk).start()

        for chunk in range(chunks):
            take(chunk)
            if chunk > 0:
                give(chunk - 1)
        give(chunks - 1)
        return carry

    lax.fori_loop(0, lanes, chain, 0)

    def send_grad(i):
        return pltpu.make_async_remote_copy(
            src_ref=grad.at[piece(peer(i))], dst_ref=gathered.at[me],
            send_sem=grad_send.at[peer(i)], recv_sem=grad_recv.at[me],
            device_id={"freq": peer(i)}, device_id_type=MESH,
        )

    def recv_grad(i):
        return pltpu.make_async_remote_copy(
            src_ref=grad.at[piece(peer(i))], dst_ref=gathered.at[peer(i)],
            send_sem=grad_send.at[peer(i)], recv_sem=grad_recv.at[peer(i)],
            device_id={"freq": peer(i)}, device_id_type=MESH,
        )

    def start_grad(i, carry):
        send_grad(i).start()
        return carry

    lax.fori_loop(1, peers, start_grad, 0)
    gathered[me] = grad[piece(me)]

    def wait_grad(i, carry):
        recv_grad(i).wait_recv()
        return carry

    lax.fori_loop(1, peers, wait_grad, 0)

    def add(i, total):
        return total + gathered[i]

    total = lax.fori_loop(0, peers, add, jnp.zeros(out_ref.shape, jnp.float32))
    out_ref[...] = total * (1.0 / count)

    def drain(i, carry):
        send_slow(i).wait_send()
        send_grad(i).wait_send()
        return carry

    lax.fori_loop(1, peers, drain, 0)

    @pl.when(d > 0)
    def _():
        def drain_mu(i, carry):
            hop(i // chunks, i % chunks).wait_send()
            return carry

        lax.fori_loop(0, lanes * chunks, drain_mu, 0)


def on_device(slowness, freq_index, taps, source_top, adjoint_source):
    lanes, _, _, lines, cells = source_top.shape
    peers, depths = lax.axis_size("freq"), lax.axis_size("depth")
    count, _, width = taps.shape
    reach = width // 2
    assert cells == SUB * LANES and slowness.shape[0] == 1
    rows = slowness.shape[1] // LANES
    whole_lines = rows % SUB == 0
    piece = (rows // SUB, SUB, LANES) if whole_lines else (1, rows, LANES)
    pieces = (piece[0] * peers,) + piece[1:]
    line = (SUB, LANES)
    f32 = jnp.float32
    vmem = pl.BlockSpec(memory_space=pltpu.VMEM)
    smem = pl.BlockSpec(memory_space=pltpu.SMEM)
    hbm = pl.BlockSpec(memory_space=pl.ANY)
    dma = pltpu.SemaphoreType.DMA
    chunks = lines // CHUNK
    out = pl.pallas_call(
        functools.partial(
            kernel, peers, depths, lanes, lines, reach, count, piece[0], whole_lines
        ),
        out_shape=jax.ShapeDtypeStruct(piece, f32),
        in_specs=[vmem, smem, smem, hbm, hbm],
        out_specs=vmem,
        scratch_shapes=[
            pltpu.VMEM((lanes, 2, lines, cells), f32),
            pltpu.VMEM((lanes, 2, lines, cells), f32),
            pltpu.VMEM((lanes, 2, lines) + line, f32),
            pltpu.VMEM((lanes, 2, lines) + line, f32),
            pltpu.VMEM((2, lines + 2 * reach) + line, f32),
            pltpu.VMEM(pieces, f32),
            pltpu.VMEM((lanes, lines) + line, f32),
            pltpu.VMEM((lanes, lines) + line, f32),
            pltpu.VMEM((lanes, lines, 2) + line, f32),
            pltpu.VMEM((lanes, lines, 2) + line, f32),
            pltpu.VMEM(pieces, f32),
            pltpu.VMEM((peers,) + piece, f32),
            dma((2,)),
            dma((peers,)),
            dma((peers,)),
            dma((lanes * chunks,)),
            dma((lanes * chunks,)),
            dma((peers,)),
            dma((peers,)),
        ],
        compiler_params=pltpu.CompilerParams(
            collective_id=0, has_side_effects=True, vmem_limit_bytes=56 * 1024 * 1024
        ),
    )(
        slowness.reshape(piece),
        freq_index,
        taps.transpose(2, 1, 0),
        source_top.reshape(lanes, 2, lines, cells),
        adjoint_source.reshape(lanes, 2, lines, cells),
    )
    return out.reshape(slowness.shape)


def solution(mesh):
    in_specs = (
        P("depth", "freq"),
        P("freq"),
        P(),
        P("freq", "depth", None, None, None),
        P("freq", "depth", None, None, None),
    )
    out_specs = P("depth", "freq")
    return jax.shard_map(
        on_device, mesh=mesh, in_specs=in_specs, out_specs=out_specs, check_vma=False
    )
```

time: 324 us -> 28.3 us (0.09)
  waiting for transfers between devices: 230 us -> 0 us
  blocking collectives: 32.5 us -> 0 us
  Pallas kernels: 0 us -> 26.6 us
  local copies, waits for them, and re-layouts: 23.4 us -> 1.31 us
  other arithmetic: 19.5 us -> 0 us
  between operations: 13.5 us -> 0.01 us
  starting transfers between devices: 3.88 us -> 0 us
    unnamed x2 -> x0, waiting for transfers between devices: 213 us -> none
    all_gather x1 -> x0, blocking collectives: 32.5 us -> none  [on_device(): lax.all_gather(slowness, 'freq', axis=1, tiled=True)]
    pallas_call x0 -> x1, Pallas kernels: none -> 26.6 us  [on_device(): pl.pallas_call(functools.partial(kernel, peers, depths, lanes, lines, rea...]
    unnamed x10 -> x1, local copies, waits for them, and re-layouts: 20.8 us -> 1.31 us
    ppermute x3 -> x0, waiting for transfers between devices: 17.3 us -> none  [from_behind(): lax.ppermute(value, axis, [(source, source + steps) for source in range(l...]
    another operation x9 -> x0, other arithmetic: 6.86 us -> none  [sweep(): return (jnp.stack(carry, axis=1), jnp.stack(terms))]
    add x7 -> x0, other arithmetic: 5.5 us -> none  [the longest x3 2.43 us: adjoint_step(): mid_re = phase_cos * field_re + phase_sin * field_im]
    ppermute x3 -> x0, starting transfers between devices: 3.88 us -> none  [from_behind(): lax.ppermute(value, axis, [(source, source + steps) for source in range(l...]
  transfers between devices with their start and end apart: 4 -> 0, of which waited for: 4 -> 0; matrix products, arithmetic and copies ran while one was open for 0% -> 0% of each run, Pallas kernels for 0% -> 0%
where the time goes in v1:
time: 28.3 us; the launch traced here: 28 us
  Pallas kernels  26.6 us (94%)
  local copies, waits for them, and re-layouts  1.31 us (5%)
    pallas_call x1, Pallas kernels, on_device(): pl.pallas_call(functools.partial(kernel, peers, depths, lanes, lines, rea...  26.6 us
    unnamed x1, local copies, waits for them, and re-layouts  1.31 us

profile of v1, /device:TPU:0, one launch (start us, length us, event | category | flops | bytes accessed | tf_op | source)
XLA Modules:
  0.0 28.0 jit_solution(14472589478347322810)
XLA Ops:
  0.0 26.6 %shard_map.55 = f32[3,8,128]{2,1,0:T(8,128)} custom-call(f32[3,8,128]{2,1,0:T(8,128)} %bitcast.8, s32[2]{0:T(128)} %index_ref.1, f32[11,2,16]{2,1,0:T(2,128)} %bitcast.9, f32[2,2,24,1024]{3,2,1,0:T(8,128)} %bitcast.5, f32[2,2,24,1024]{3,2,1,0:T(8,128)} %bitcast.6), custom_call_target="tpu_custom_call" | custom-call | tf_op jit(solution)/shard_map/pallas_call | solution.py:348
  26.7 1.3 %copy.7 = f32[1,3072]{1,0:T(1,128)} copy(f32[1,3072]{1,0:T(1,128)} %bitcast.7) | data formatting | bytes 24576

commit v2 on v1

v2 whole, which is shorter than its diff:
```python
import functools
import math

import jax
import jax.numpy as jnp
from jax import lax
from jax.experimental import pallas as pl
from jax.experimental.pallas import tpu as pltpu
from jax.sharding import PartitionSpec as P

MESH = pl.DeviceIdType.MESH
LANES = 128
SUB = 8
BLOCK = 4
CHUNK = 8

PI_HIGH = 3.140625
PI_LOW = math.pi - PI_HIGH


def sin_cos(phase):
    turns = jnp.floor(phase * (1.0 / math.pi) + 0.5)
    rest = (phase - turns * PI_HIGH) - turns * PI_LOW
    sign = 1.0 - 2.0 * (turns - 2.0 * jnp.floor(turns * 0.5))
    square = rest * rest
    odd = -1.0 / math.factorial(11)
    for n, s in ((9, 1), (7, -1), (5, 1), (3, -1), (1, 1)):
        odd = odd * square + s / math.factorial(n)
    even = 1.0 / math.factorial(12)
    for n, s in ((10, -1), (8, 1), (6, -1), (4, 1), (2, -1), (0, 1)):
        even = even * square + s / math.factorial(n)
    return sign * rest * odd, sign * even


def shifted(value, reach):
    lane = lax.broadcasted_iota(jnp.int32, value.shape, 2)
    row = lax.broadcasted_iota(jnp.int32, value.shape, 1)
    after = jnp.where(row < SUB - 1, pltpu.roll(value, SUB - 1, 1), 0.0)
    before = jnp.where(row > 0, pltpu.roll(value, 1, 1), 0.0)
    out = {0: value}
    for o in range(1, reach + 1):
        out[o] = pltpu.roll(jnp.where(lane >= o, value, after), LANES - o, 2)
        out[-o] = pltpu.roll(jnp.where(lane < LANES - o, value, before), o, 2)
    return out


def filtered(at_re, at_im, taps, adjoint):
    reach = len(taps) // 2
    out_re = out_im = None
    for k, (t_re, t_im) in enumerate(taps):
        o = reach - k if adjoint else k - reach
        u_re, u_im = at_re(o), at_im(o)
        if adjoint:
            t_im = -t_im
        add_re = t_re * u_re - t_im * u_im
        add_im = t_re * u_im + t_im * u_re
        out_re = add_re if out_re is None else out_re + add_re
        out_im = add_im if out_im is None else out_im + add_im
    return out_re, out_im


def filter_x(re, im, taps, adjoint):
    reach = len(taps) // 2
    all_re, all_im = shifted(re, reach), shifted(im, reach)
    return filtered(lambda o: all_re[o], lambda o: all_im[o], taps, adjoint)


def kernel(
    peers, depths, lanes, lines, reach, count, per_piece, whole_lines,
    slow_hbm, index_hbm, taps_hbm, source_hbm, adjoint_hbm, out_ref,
    slow_ref, index_ref, taps_ref, source_in, adjoint_in, wave, adj, padded, slow, cosine, sine,
    arrived, leaving, grad, gathered,
    in_sem, slow_send, slow_recv, mu_send, mu_recv, grad_send, grad_recv,
):
    me = lax.axis_index("freq")
    d = lax.axis_index("depth")
    chunks = lines // CHUNK
    per_line = max(1, peers // lines)

    load_slow = pltpu.make_async_copy(slow_hbm, slow_ref, in_sem.at[0])
    load_index = pltpu.make_async_copy(index_hbm, index_ref, in_sem.at[1])
    load_taps = pltpu.make_async_copy(taps_hbm, taps_ref, in_sem.at[2])
    load_adjoint = pltpu.make_async_copy(adjoint_hbm, adjoint_in, in_sem.at[3])
    load_source = pltpu.make_async_copy(source_hbm, source_in, in_sem.at[4])

    barrier = pltpu.get_barrier_semaphore()

    def peer(i):
        return lax.rem(me + i, peers)

    def greet(i, carry):
        pl.semaphore_signal(barrier, inc=1, device_id={"freq": peer(i)}, device_id_type=MESH)
        return carry

    lax.fori_loop(1, peers, greet, 0)

    @pl.when(d < depths - 1)
    def _():
        pl.semaphore_signal(barrier, inc=1, device_id={"depth": d + 1}, device_id_type=MESH)

    for load in (load_slow, load_index, load_taps, load_adjoint, load_source):
        load.start()

    def piece(i):
        return pl.ds(i * per_piece, per_piece)

    margin = jnp.zeros((reach, SUB, LANES), jnp.float32)
    for part in range(2):
        padded[part, pl.ds(0, reach)] = margin
        padded[part, pl.ds(lines + reach, reach)] = margin
    grad[...] = jnp.zeros_like(grad)

    @pl.when(d == depths - 1)
    def _():
        arrived[...] = jnp.zeros_like(arrived)

    load_slow.wait()
    slow[piece(me)] = slow_ref[...]
    pl.semaphore_wait(barrier, jnp.where(d > 0, peers, peers - 1))

    def push_slow(i, sender):
        return pltpu.make_async_remote_copy(
            src_ref=slow_ref, dst_ref=slow.at[piece(sender)],
            send_sem=slow_send.at[peer(i)], recv_sem=slow_recv.at[sender],
            device_id={"freq": peer(i)}, device_id_type=MESH,
        )

    def start_slow(i, carry):
        push_slow(i, me).start()
        return carry

    lax.fori_loop(1, peers, start_slow, 0)
    load_index.wait()
    load_taps.wait()

    def wait_slow(i, carry):
        push_slow(i, peer(i)).wait_recv()
        return carry

    def tap_list(f):
        row = index_ref[f]
        return [(taps_ref[k, 0, row], taps_ref[k, 1, row]) for k in range(2 * reach + 1)]

    def angular(f):
        return 8.0 * (index_ref[f].astype(jnp.float32) + 1.0) / count

    def block(y):
        return pl.ds(y, BLOCK)

    def each_block(first, last, body):
        def step(b, carry):
            body(b * BLOCK)
            return carry

        lax.fori_loop(first // BLOCK, last // BLOCK, step, 0)

    def each_lane(body):
        def step(f, carry):
            body(f)
            return carry

        lax.fori_loop(0, lanes, step, 0)

    def unfold(from_ref, to_ref):
        def body(i, carry):
            f, part = i // 2, i % 2
            for t in range(lines // SUB):
                rows = from_ref[f, part, pl.ds(t * SUB, SUB), :]
                to_ref[f, part, pl.ds(t * SUB, SUB)] = rows.reshape(SUB, SUB, LANES)
            return carry

        lax.fori_loop(0, 2 * lanes, body, 0)

    def filter_y(y, taps, adjoint):
        return filtered(
            lambda o: padded[0, block(y + reach + o)],
            lambda o: padded[1, block(y + reach + o)],
            taps, adjoint,
        )

    def slow_block(y):
        if whole_lines:
            return slow[block(y)]
        return slow[pl.ds(y * per_line, BLOCK * per_line)].reshape(BLOCK, SUB, LANES)

    def add_grad(y, term):
        if whole_lines:
            grad[block(y)] += term
        else:
            grad[pl.ds(y * per_line, BLOCK * per_line)] += term.reshape(
                BLOCK * per_line, SUB // per_line, LANES
            )

    def phases(f):
        w = angular(f)

        def body(y):
            s, co = sin_cos(w * slow_block(y))
            sine[f, block(y)] = s
            cosine[f, block(y)] = co

        each_block(0, lines, body)

    def forward(f, finish):
        taps = tap_list(f)

        def along_x(y):
            re, im = filter_x(wave[f, 0, block(y)], wave[f, 1, block(y)], taps, False)
            padded[0, block(y + reach)] = re
            padded[1, block(y + reach)] = im

        def along_y(y):
            finish(f, y, *filter_y(y, taps, False))

        each_block(0, lines, along_x)
        each_block(0, lines, along_y)

    def turned(f, y, re, im):
        w, co, s = angular(f), cosine[f, block(y)], sine[f, block(y)]
        return w * (co * re - s * im), w * (s * re + co * im)

    def hop(f, chunk):
        rows = pl.ds(chunk * CHUNK, CHUNK)
        slot = f * chunks + chunk
        return pltpu.make_async_remote_copy(
            src_ref=leaving.at[f, rows], dst_ref=arrived.at[f, rows],
            send_sem=mu_send.at[slot], recv_sem=mu_recv.at[slot],
            device_id={"depth": lax.max(d - 1, 0)}, device_id_type=MESH,
        )

    def chain(f, use):
        taps = tap_list(f)

        def take(chunk):
            @pl.when(d < depths - 1)
            def _():
                hop(f, chunk).wait_recv()

            def body(y):
                mu_re = adj[f, 0, block(y)] + arrived[f, block(y), 0]
                mu_im = adj[f, 1, block(y)] + arrived[f, block(y), 1]
                use(f, y, mu_re, mu_im)
                co, s = cosine[f, block(y)], sine[f, block(y)]
                padded[0, block(y + reach)] = co * mu_re + s * mu_im
                padded[1, block(y + reach)] = co * mu_im - s * mu_re

            each_block(chunk * CHUNK, (chunk + 1) * CHUNK, body)

        def give(chunk):
            @pl.when(d > 0)
            def _():
                def body(y):
                    re, im = filter_y(y, taps, True)
                    re, im = filter_x(re, im, taps, True)
                    leaving[f, block(y), 0] = re
                    leaving[f, block(y), 1] = im

                each_block(chunk * CHUNK, (chunk + 1) * CHUNK, body)
                hop(f, chunk).start()

        for chunk in range(chunks):
            take(chunk)
            if chunk > 0:
                give(chunk - 1)
        give(chunks - 1)

    def push_grad(to, sender):
        return pltpu.make_async_remote_copy(
            src_ref=grad.at[piece(to)], dst_ref=gathered.at[sender],
            send_sem=grad_send.at[to], recv_sem=grad_recv.at[sender],
            device_id={"freq": to}, device_id_type=MESH,
        )

    def send_grad(first, last):
        def step(to, carry):
            @pl.when(to != me)
            def _():
                push_grad(to, me).start()

            return carry

        lax.fori_loop(first, last, step, 0)

    early = d >= depths // 2

    @pl.when(early)
    def _():
        load_adjoint.wait()
        unfold(adjoint_in, adj)
        lax.fori_loop(1, peers, wait_slow, 0)

        def keep(f, y, mu_re, mu_im):
            adj[f, 0, block(y)] = mu_re
            adj[f, 1, block(y)] = mu_im

        def first(f):
            phases(f)
            chain(f, keep)

        each_lane(first)
        load_source.wait()
        unfold(source_in, wave)

        def finish(f, y, re, im):
            re, im = turned(f, y, re, im)
            add_grad(y, adj[f, 1, block(y)] * re - adj[f, 0, block(y)] * im)

        each_lane(lambda f: forward(f, finish))
        send_grad(0, peers)

    @pl.when(jnp.logical_not(early))
    def _():
        load_source.wait()
        unfold(source_in, wave)

        def finish(f, y, re, im):
            wave[f, 0, block(y)] = re
            wave[f, 1, block(y)] = im

        each_lane(lambda f: forward(f, finish))
        load_adjoint.wait()
        unfold(adjoint_in, adj)
        lax.fori_loop(1, peers, wait_slow, 0)

        def turn(f):
            phases(f)

            def body(y):
                re, im = turned(f, y, wave[f, 0, block(y)], wave[f, 1, block(y)])
                wave[f, 0, block(y)] = re
                wave[f, 1, block(y)] = im

            each_block(0, lines, body)

        each_lane(turn)

        def use(f, y, mu_re, mu_im):
            add_grad(y, mu_im * wave[f, 0, block(y)] - mu_re * wave[f, 1, block(y)])

        each_lane(lambda f: chain(f, use))
        send_grad(0, peers)

    gathered[me] = grad[piece(me)]

    def add(i, total):
        push_grad(me, peer(i)).wait_recv()
        return total + gathered[peer(i)]

    total = lax.fori_loop(1, peers, add, gathered[me])
    out_ref[...] = total * (1.0 / count)

    def drain(i, carry):
        push_slow(i, me).wait_send()
        push_grad(peer(i), me).wait_send()
        return carry

    lax.fori_loop(1, peers, drain, 0)

    @pl.when(d > 0)
    def _():
        def drain_mu(i, carry):
            hop(i // chunks, i % chunks).wait_send()
            return carry

        lax.fori_loop(0, lanes * chunks, drain_mu, 0)


def on_device(slowness, freq_index, taps, source_top, adjoint_source):
    lanes, _, _, lines, cells = source_top.shape
    peers, depths = lax.axis_size("freq"), lax.axis_size("depth")
    count, _, width = taps.shape
    reach = width // 2
    assert cells == SUB * LANES and slowness.shape[0] == 1
    rows = slowness.shape[1] // LANES
    whole_lines = rows % SUB == 0
    piece = (rows // SUB, SUB, LANES) if whole_lines else (1, rows, LANES)
    pieces = (piece[0] * peers,) + piece[1:]
    line = (SUB, LANES)
    f32 = jnp.float32
    vmem = pl.BlockSpec(memory_space=pltpu.VMEM)
    hbm = pl.BlockSpec(memory_space=pl.ANY)
    dma = pltpu.SemaphoreType.DMA
    chunks = lines // CHUNK
    out = pl.pallas_call(
        functools.partial(
            kernel, peers, depths, lanes, lines, reach, count, piece[0], whole_lines
        ),
        out_shape=jax.ShapeDtypeStruct(piece, f32),
        in_specs=[hbm] * 5,
        out_specs=vmem,
        scratch_shapes=[
            pltpu.VMEM(piece, f32),
            pltpu.SMEM((lanes,), jnp.int32),
            pltpu.SMEM((width, 2, count), f32),
            pltpu.VMEM((lanes, 2, lines, cells), f32),
            pltpu.VMEM((lanes, 2, lines, cells), f32),
            pltpu.VMEM((lanes, 2, lines) + line, f32),
            pltpu.VMEM((lanes, 2, lines) + line, f32),
            pltpu.VMEM((2, lines + 2 * reach) + line, f32),
            pltpu.VMEM(pieces, f32),
            pltpu.VMEM((lanes, lines) + line, f32),
            pltpu.VMEM((lanes, lines) + line, f32),
            pltpu.VMEM((lanes, lines, 2) + line, f32),
            pltpu.VMEM((lanes, lines, 2) + line, f32),
            pltpu.VMEM(pieces, f32),
            pltpu.VMEM((peers,) + piece, f32),
            dma((5,)),
            dma((peers,)),
            dma((peers,)),
            dma((lanes * chunks,)),
            dma((lanes * chunks,)),
            dma((peers,)),
            dma((peers,)),
        ],
        compiler_params=pltpu.CompilerParams(
            collective_id=0, has_side_effects=True, vmem_limit_bytes=56 * 1024 * 1024
        ),
    )(
        slowness.reshape(piece),
        freq_index,
        taps.transpose(2, 1, 0),
        source_top.reshape(lanes, 2, lines, cells),
        adjoint_source.reshape(lanes, 2, lines, cells),
    )
    return out.reshape(slowness.shape)


def solution(mesh):
    in_specs = (
        P("depth", "freq"),
        P("freq"),
        P(),
        P("freq", "depth", None, None, None),
        P("freq", "depth", None, None, None),
    )
    out_specs = P("depth", "freq")
    return jax.shard_map(
        on_device, mesh=mesh, in_specs=in_specs, out_specs=out_specs, check_vma=False
    )
```

time: 28.3 us -> 27 us (0.954)
  Pallas kernels: 26.6 us -> 25.4 us
    pallas_call x1, Pallas kernels: 26.6 us -> 25.4 us  [on_device(): pl.pallas_call(functools.partial(kernel, peers, depths, lanes, lines, rea...]
where the time goes in v2:
time: 27 us; the launch traced here: 26.7 us
  Pallas kernels  25.4 us (94%)
  local copies, waits for them, and re-layouts  1.31 us (5%)
    pallas_call x1, Pallas kernels, on_device(): pl.pallas_call(functools.partial(kernel, peers, depths, lanes, lines, rea...  25.4 us
    unnamed x1, local copies, waits for them, and re-layouts  1.31 us

profile of v2, /device:TPU:0, one launch (start us, length us, event | category | flops | bytes accessed | tf_op | source)
XLA Modules:
  0.0 26.7 jit_solution(6480299565014834799)
XLA Ops:
  0.0 25.4 %shard_map.55 = f32[3,8,128]{2,1,0:T(8,128)} custom-call(f32[3,8,128]{2,1,0:T(8,128)} %bitcast.8, s32[2]{0:T(128)} %index_hbm.1, f32[11,2,16]{2,1,0:T(2,128)} %bitcast.9, f32[2,2,24,1024]{3,2,1,0:T(8,128)} %bitcast.5, f32[2,2,24,1024]{3,2,1,0:T(8,128)} %bitcast.6), custom_call_target="tpu_custom_call" | custom-call | tf_op jit(solution)/shard_map/pallas_call | solution.py:384
  25.4 1.3 %copy.7 = f32[1,3072]{1,0:T(1,128)} copy(f32[1,3072]{1,0:T(1,128)} %bitcast.7) | data formatting | bytes 24576

commit v3 on v2

--- a/solution.py
+++ b/solution.py
@@ -44,25 +44,24 @@
     return out
 
 
-def filtered(at_re, at_im, taps, adjoint):
+def filtered(at, taps, adjoint):
     reach = len(taps) // 2
-    out_re = out_im = None
+    total = None
     for k, (t_re, t_im) in enumerate(taps):
         o = reach - k if adjoint else k - reach
-        u_re, u_im = at_re(o), at_im(o)
+        u_re, u_im, u_sum = at(o)
         if adjoint:
             t_im = -t_im
-        add_re = t_re * u_re - t_im * u_im
-        add_im = t_re * u_im + t_im * u_re
-        out_re = add_re if out_re is None else out_re + add_re
-        out_im = add_im if out_im is None else out_im + add_im
-    return out_re, out_im
+        new = (t_re * u_sum, (t_im - t_re) * u_re, (t_re + t_im) * u_im)
+        total = new if total is None else tuple(x + y for x, y in zip(total, new))
+    a, b, c = total
+    return a - c, a + b
 
 
 def filter_x(re, im, taps, adjoint):
     reach = len(taps) // 2
     all_re, all_im = shifted(re, reach), shifted(im, reach)
-    return filtered(lambda o: all_re[o], lambda o: all_im[o], taps, adjoint)
+    return filtered(lambda o: (all_re[o], all_im[o], all_re[o] + all_im[o]), taps, adjoint)
 
 
 def kernel(
@@ -105,7 +104,7 @@
         return pl.ds(i * per_piece, per_piece)
 
     margin = jnp.zeros((reach, SUB, LANES), jnp.float32)
-    for part in range(2):
+    for part in range(3):
         padded[part, pl.ds(0, reach)] = margin
         padded[part, pl.ds(lines + reach, reach)] = margin
     grad[...] = jnp.zeros_like(grad)
@@ -149,10 +148,14 @@
 
     def each_block(first, last, body):
         def step(b, carry):
-            body(b * BLOCK)
+            for part in range(CHUNK // BLOCK):
+                body(b * CHUNK + part * BLOCK)
             return carry
 
-        lax.fori_loop(first // BLOCK, last // BLOCK, step, 0)
+        if last - first == CHUNK:
+            step(first // CHUNK, 0)
+        else:
+            lax.fori_loop(first // CHUNK, last // CHUNK, step, 0)
 
     def each_lane(body):
         def step(f, carry):
@@ -173,10 +176,14 @@
 
     def filter_y(y, taps, adjoint):
         return filtered(
-            lambda o: padded[0, block(y + reach + o)],
-            lambda o: padded[1, block(y + reach + o)],
+            lambda o: tuple(padded[part, block(y + reach + o)] for part in range(3)),
             taps, adjoint,
         )
+
+    def put_padded(y, re, im):
+        padded[0, block(y + reach)] = re
+        padded[1, block(y + reach)] = im
+        padded[2, block(y + reach)] = re + im
 
     def slow_block(y):
         if whole_lines:
@@ -206,8 +213,7 @@
 
         def along_x(y):
             re, im = filter_x(wave[f, 0, block(y)], wave[f, 1, block(y)], taps, False)
-            padded[0, block(y + reach)] = re
-            padded[1, block(y + reach)] = im
+            put_padded(y, re, im)
 
         def along_y(y):
             finish(f, y, *filter_y(y, taps, False))
@@ -228,7 +234,7 @@
             device_id={"depth": lax.max(d - 1, 0)}, device_id_type=MESH,
         )
 
-    def chain(f, use):
+    def chain(f, use, taken):
         taps = tap_list(f)
 
         def take(chunk):
@@ -241,8 +247,7 @@
                 mu_im = adj[f, 1, block(y)] + arrived[f, block(y), 1]
                 use(f, y, mu_re, mu_im)
                 co, s = cosine[f, block(y)], sine[f, block(y)]
-                padded[0, block(y + reach)] = co * mu_re + s * mu_im
-                padded[1, block(y + reach)] = co * mu_im - s * mu_re
+                put_padded(y, co * mu_re + s * mu_im, co * mu_im - s * mu_re)
 
             each_block(chunk * CHUNK, (chunk + 1) * CHUNK, body)
 
@@ -260,6 +265,7 @@
 
         for chunk in range(chunks):
             take(chunk)
+            taken(f, chunk)
             if chunk > 0:
                 give(chunk - 1)
         give(chunks - 1)
@@ -295,7 +301,7 @@
 
         def first(f):
             phases(f)
-            chain(f, keep)
+            chain(f, keep, lambda f, chunk: None)
 
         each_lane(first)
         load_source.wait()
@@ -337,8 +343,13 @@
         def use(f, y, mu_re, mu_im):
             add_grad(y, mu_im * wave[f, 0, block(y)] - mu_re * wave[f, 1, block(y)])
 
-        each_lane(lambda f: chain(f, use))
-        send_grad(0, peers)
+        def taken(f, chunk):
+            @pl.when(f == lanes - 1)
+            def _():
+                done = [n * CHUNK * peers // lines for n in (chunk, chunk + 1)]
+                send_grad(*done)
+
+        each_lane(lambda f: chain(f, use, taken))
 
     gathered[me] = grad[piece(me)]
 
@@ -378,7 +389,7 @@
     line = (SUB, LANES)
     f32 = jnp.float32
     vmem = pl.BlockSpec(memory_space=pltpu.VMEM)
-    hbm = pl.BlockSpec(memory_space=pl.ANY)
+    hbm = pl.BlockSpec(memory_space=pltpu.HBM)
     dma = pltpu.SemaphoreType.DMA
     chunks = lines // CHUNK
     out = pl.pallas_call(
@@ -396,7 +407,7 @@
             pltpu.VMEM((lanes, 2, lines, cells), f32),
             pltpu.VMEM((lanes, 2, lines) + line, f32),
             pltpu.VMEM((lanes, 2, lines) + line, f32),
-            pltpu.VMEM((2, lines + 2 * reach) + line, f32),
+            pltpu.VMEM((3, lines + 2 * reach) + line, f32),
             pltpu.VMEM(pieces, f32),
             pltpu.VMEM((lanes, lines) + line, f32),
             pltpu.VMEM((lanes, lines) + line, f32),

time: 27 us -> 25.5 us (0.944)
  Pallas kernels: 25.4 us -> 23.9 us
    pallas_call x1, Pallas kernels: 25.4 us -> 23.9 us  [on_device(): pl.pallas_call(functools.partial(kernel, peers, depths, lanes, lines, rea...]
where the time goes in v3:
time: 25.5 us; the launch traced here: 25.2 us
  Pallas kernels  23.9 us (94%)
  local copies, waits for them, and re-layouts  1.31 us (5%)
    pallas_call x1, Pallas kernels, on_device(): pl.pallas_call(functools.partial(kernel, peers, depths, lanes, lines, rea...  23.9 us
    unnamed x1, local copies, waits for them, and re-layouts  1.31 us

profile of v3, /device:TPU:0, one launch (start us, length us, event | category | flops | bytes accessed | tf_op | source)
XLA Modules:
  0.0 25.2 jit_solution(12415160316851742691)
XLA Ops:
  0.0 23.9 %shard_map.55 = f32[3,8,128]{2,1,0:T(8,128)} custom-call(f32[3,8,128]{2,1,0:T(8,128)} %bitcast.8, s32[2]{0:T(128)} %index_hbm.1, f32[11,2,16]{2,1,0:T(2,128)} %bitcast.9, f32[2,2,24,1024]{3,2,1,0:T(8,128)} %bitcast.5, f32[2,2,24,1024]{3,2,1,0:T(8,128)} %bitcast.6), custom_call_target="tpu_custom_call" | custom-call | tf_op jit(solution)/shard_map/pallas_call | solution.py:395
  23.9 1.3 %copy.7 = f32[1,3072]{1,0:T(1,128)} copy(f32[1,3072]{1,0:T(1,128)} %bitcast.7) | data formatting | bytes 24576

commit v4 on v3

--- a/solution.py
+++ b/solution.py
@@ -12,7 +12,8 @@
 LANES = 128
 SUB = 8
 BLOCK = 4
-CHUNK = 8
+STEP = 8
+CHUNK = 4
 
 PI_HIGH = 3.140625
 PI_LOW = math.pi - PI_HIGH
@@ -147,15 +148,17 @@
         return pl.ds(y, BLOCK)
 
     def each_block(first, last, body):
+        if last - first <= STEP:
+            for y in range(first, last, BLOCK):
+                body(y)
+            return
+
         def step(b, carry):
-            for part in range(CHUNK // BLOCK):
-                body(b * CHUNK + part * BLOCK)
+            for part in range(STEP // BLOCK):
+                body(b * STEP + part * BLOCK)
             return carry
 
-        if last - first == CHUNK:
-            step(first // CHUNK, 0)
-        else:
-            lax.fori_loop(first // CHUNK, last // CHUNK, step, 0)
+        lax.fori_loop(first // STEP, last // STEP, step, 0)
 
     def each_lane(body):
         def step(f, carry):
@@ -198,7 +201,7 @@
                 BLOCK * per_line, SUB // per_line, LANES
             )
 
-    def phases(f):
+    def phases(f, first=0, last=lines):
         w = angular(f)
 
         def body(y):
@@ -206,7 +209,7 @@
             sine[f, block(y)] = s
             cosine[f, block(y)] = co
 
-        each_block(0, lines, body)
+        each_block(first, last, body)
 
     def forward(f, finish):
         taps = tap_list(f)
@@ -234,29 +237,42 @@
             device_id={"depth": lax.max(d - 1, 0)}, device_id_type=MESH,
         )
 
-    def chain(f, use, taken):
+    def chain(f, before, use, taken, x_first):
         taps = tap_list(f)
+        lag = -(-reach // CHUNK)
 
         def take(chunk):
             @pl.when(d < depths - 1)
             def _():
                 hop(f, chunk).wait_recv()
 
-            def body(y):
-                mu_re = adj[f, 0, block(y)] + arrived[f, block(y), 0]
-                mu_im = adj[f, 1, block(y)] + arrived[f, block(y), 1]
-                use(f, y, mu_re, mu_im)
-                co, s = cosine[f, block(y)], sine[f, block(y)]
-                put_padded(y, co * mu_re + s * mu_im, co * mu_im - s * mu_re)
-
-            each_block(chunk * CHUNK, (chunk + 1) * CHUNK, body)
+            before(f, chunk)
+            first, last = chunk * CHUNK, (chunk + 1) * CHUNK
+
+            def mu(y):
+                return adj[f, 0, block(y)] + arrived[f, block(y), 0], adj[f, 1, block(y)] + arrived[f, block(y), 1]
+
+            @pl.when(d > 0)
+            def _():
+                def body(y):
+                    mu_re, mu_im = mu(y)
+                    co, s = cosine[f, block(y)], sine[f, block(y)]
+                    re, im = co * mu_re + s * mu_im, co * mu_im - s * mu_re
+                    if x_first:
+                        re, im = filter_x(re, im, taps, True)
+                    put_padded(y, re, im)
+
+                each_block(first, last, body)
+
+            each_block(first, last, lambda y: use(f, y, *mu(y)))
 
         def give(chunk):
             @pl.when(d > 0)
             def _():
                 def body(y):
                     re, im = filter_y(y, taps, True)
-                    re, im = filter_x(re, im, taps, True)
+                    if not x_first:
+                        re, im = filter_x(re, im, taps, True)
                     leaving[f, block(y), 0] = re
                     leaving[f, block(y), 1] = im
 
@@ -265,10 +281,13 @@
 
         for chunk in range(chunks):
             take(chunk)
-            taken(f, chunk)
-            if chunk > 0:
-                give(chunk - 1)
-        give(chunks - 1)
+            if chunk >= lag:
+                give(chunk - lag)
+            if chunk < chunks - 1:
+                taken(f, chunk)
+        for chunk in range(chunks - lag, chunks):
+            give(chunk)
+        taken(f, chunks - 1)
 
     def push_grad(to, sender):
         return pltpu.make_async_remote_copy(
@@ -299,11 +318,16 @@
             adj[f, 0, block(y)] = mu_re
             adj[f, 1, block(y)] = mu_im
 
-        def first(f):
-            phases(f)
-            chain(f, keep, lambda f, chunk: None)
-
-        each_lane(first)
+        @pl.when(d < depths - 1)
+        def _():
+            each_lane(phases)
+
+        def before(f, chunk):
+            @pl.when(d == depths - 1)
+            def _():
+                phases(f, chunk * CHUNK, (chunk + 1) * CHUNK)
+
+        each_lane(lambda f: chain(f, before, keep, lambda f, chunk: None, False))
         load_source.wait()
         unfold(source_in, wave)
 
@@ -349,7 +373,7 @@
                 done = [n * CHUNK * peers // lines for n in (chunk, chunk + 1)]
                 send_grad(*done)
 
-        each_lane(lambda f: chain(f, use, taken))
+        each_lane(lambda f: chain(f, lambda f, chunk: None, use, taken, True))
 
     gathered[me] = grad[piece(me)]
 

time: 25.5 us -> 25.1 us (0.984)
  Pallas kernels: 23.9 us -> 23.5 us
    pallas_call x1, Pallas kernels: 23.9 us -> 23.5 us  [on_device(): pl.pallas_call(functools.partial(kernel, peers, depths, lanes, lines, rea...]
where the time goes in v4:
time: 25.1 us; the launch traced here: 24.8 us
  Pallas kernels  23.5 us (94%)
  local copies, waits for them, and re-layouts  1.31 us (5%)
    pallas_call x1, Pallas kernels, on_device(): pl.pallas_call(functools.partial(kernel, peers, depths, lanes, lines, rea...  23.5 us
    unnamed x1, local copies, waits for them, and re-layouts  1.31 us

profile of v4, /device:TPU:0, one launch (start us, length us, event | category | flops | bytes accessed | tf_op | source)
XLA Modules:
  0.0 24.8 jit_solution(17211670820972205762)
XLA Ops:
  0.0 23.5 %shard_map.55 = f32[3,8,128]{2,1,0:T(8,128)} custom-call(f32[3,8,128]{2,1,0:T(8,128)} %bitcast.8, s32[2]{0:T(128)} %index_hbm.1, f32[11,2,16]{2,1,0:T(2,128)} %bitcast.9, f32[2,2,24,1024]{3,2,1,0:T(8,128)} %bitcast.5, f32[2,2,24,1024]{3,2,1,0:T(8,128)} %bitcast.6), custom_call_target="tpu_custom_call" | custom-call | tf_op jit(solution)/shard_map/pallas_call | solution.py:419
  23.5 1.3 %copy.7 = f32[1,3072]{1,0:T(1,128)} copy(f32[1,3072]{1,0:T(1,128)} %bitcast.7) | data formatting | bytes 24576

commit v5 on v4

v5 whole, which is shorter than its diff:
```python
import functools
import math

import jax
import jax.numpy as jnp
from jax import lax
from jax.experimental import pallas as pl
from jax.experimental.pallas import tpu as pltpu
from jax.sharding import PartitionSpec as P

MESH = pl.DeviceIdType.MESH
LANES = 128
SUB = 8
BLOCK = 4
STEP = 8
CHUNK = 4

PI_HIGH = 3.140625
PI_LOW = math.pi - PI_HIGH


def sin_cos(phase):
    turns = jnp.floor(phase * (1.0 / math.pi) + 0.5)
    rest = (phase - turns * PI_HIGH) - turns * PI_LOW
    sign = 1.0 - 2.0 * (turns - 2.0 * jnp.floor(turns * 0.5))
    square = rest * rest
    odd = -1.0 / math.factorial(11)
    for n, s in ((9, 1), (7, -1), (5, 1), (3, -1), (1, 1)):
        odd = odd * square + s / math.factorial(n)
    even = 1.0 / math.factorial(12)
    for n, s in ((10, -1), (8, 1), (6, -1), (4, 1), (2, -1), (0, 1)):
        even = even * square + s / math.factorial(n)
    return sign * rest * odd, sign * even


def shifted(value, reach):
    lane = lax.broadcasted_iota(jnp.int32, value.shape, 2)
    row = lax.broadcasted_iota(jnp.int32, value.shape, 1)
    after = jnp.where(row < SUB - 1, pltpu.roll(value, SUB - 1, 1), 0.0)
    before = jnp.where(row > 0, pltpu.roll(value, 1, 1), 0.0)
    out = {0: value}
    for o in range(1, reach + 1):
        out[o] = pltpu.roll(jnp.where(lane >= o, value, after), LANES - o, 2)
        out[-o] = pltpu.roll(jnp.where(lane < LANES - o, value, before), o, 2)
    return out


def filtered(at, taps, adjoint):
    reach = len(taps) // 2
    total = None
    for k, (t_re, t_im) in enumerate(taps):
        o = reach - k if adjoint else k - reach
        u_re, u_im, u_sum = at(o)
        if adjoint:
            t_im = -t_im
        new = (t_re * u_sum, (t_im - t_re) * u_re, (t_re + t_im) * u_im)
        total = new if total is None else tuple(x + y for x, y in zip(total, new))
    a, b, c = total
    return a - c, a + b


def filter_x(re, im, taps, adjoint):
    reach = len(taps) // 2
    all_re, all_im = shifted(re, reach), shifted(im, reach)
    return filtered(lambda o: (all_re[o], all_im[o], all_re[o] + all_im[o]), taps, adjoint)


def kernel(
    peers, depths, lines, reach, count, per_piece, whole_lines,
    slow_hbm, index_hbm, taps_hbm, source_hbm, adjoint_hbm, out_ref,
    slow_ref, index_ref, taps_ref, source_in, adjoint_in, wave, adj, padded, slow, cosine, sine,
    arrived, leaving, carried, grad, gathered,
    in_sem, pair_send, pair_recv, slow_send, slow_recv, mu_send, mu_recv, grad_send, grad_recv,
):
    d = lax.axis_index("depth")
    core = d % 2
    base = d - core
    members = 2 * peers
    me = lax.axis_index("freq") * 2 + core
    chunks = lines // CHUNK
    per_line = max(1, peers // lines)
    from_below = d < depths - 2
    to_above = d >= 2

    load_slow = pltpu.make_async_copy(slow_hbm, slow_ref, in_sem.at[0])
    load_index = pltpu.make_async_copy(index_hbm, index_ref, in_sem.at[1])
    load_taps = pltpu.make_async_copy(taps_hbm, taps_ref, in_sem.at[2])
    load_adjoint = pltpu.make_async_copy(adjoint_hbm.at[core], adjoint_in.at[core], in_sem.at[3])
    load_source = pltpu.make_async_copy(source_hbm.at[core], source_in.at[core], in_sem.at[4])

    barrier = pltpu.get_barrier_semaphore()

    def other(i):
        return lax.rem(me + i, members)

    def device(member):
        return {"freq": member // 2, "depth": base + member % 2}

    def greet(i, carry):
        pl.semaphore_signal(barrier, inc=1, device_id=device(other(i)), device_id_type=MESH)
        return carry

    lax.fori_loop(1, members, greet, 0)

    @pl.when(from_below)
    def _():
        pl.semaphore_signal(barrier, inc=1, device_id={"depth": d + 2}, device_id_type=MESH)

    for load in (load_slow, load_index, load_taps, load_adjoint, load_source):
        load.start()

    def piece(i):
        return pl.ds(i * per_piece, per_piece)

    margin = jnp.zeros((reach, SUB, LANES), jnp.float32)
    for section in range(2):
        for part in range(3):
            padded[section, part, pl.ds(0, reach)] = margin
            padded[section, part, pl.ds(lines + reach, reach)] = margin
    grad[...] = jnp.zeros_like(grad)

    @pl.when(jnp.logical_not(from_below))
    def _():
        arrived[...] = jnp.zeros_like(arrived)

    load_slow.wait()
    slow[core, piece(me // 2)] = slow_ref[...]
    pl.semaphore_wait(barrier, jnp.where(to_above, members, members - 1))

    def push_slow(i, sender):
        return pltpu.make_async_remote_copy(
            src_ref=slow_ref, dst_ref=slow.at[sender % 2, piece(sender // 2)],
            send_sem=slow_send.at[other(i)], recv_sem=slow_recv.at[sender],
            device_id=device(other(i)), device_id_type=MESH,
        )

    def start_slow(i, carry):
        push_slow(i, me).start()
        return carry

    def push_pair(n, from_ref, to_ref, section):
        return pltpu.make_async_remote_copy(
            src_ref=from_ref.at[1 - core], dst_ref=to_ref.at[section],
            send_sem=pair_send.at[n], recv_sem=pair_recv.at[n],
            device_id={"depth": base + 1 - core}, device_id_type=MESH,
        )

    lax.fori_loop(1, members, start_slow, 0)
    push_pair(0, adjoint_hbm, adjoint_in, core).start()
    push_pair(1, source_hbm, source_in, core).start()
    load_index.wait()
    load_taps.wait()

    def wait_slow(i, carry):
        push_slow(i, other(i)).wait_recv()
        return carry

    row = index_ref[core]
    taps = [(taps_ref[k, 0, row], taps_ref[k, 1, row]) for k in range(2 * reach + 1)]
    w = 8.0 * (row.astype(jnp.float32) + 1.0) / count

    def block(y):
        return pl.ds(y, BLOCK)

    def each_block(first, last, body):
        if last - first <= STEP:
            for y in range(first, last, BLOCK):
                body(y)
            return

        def step(b, carry):
            for part in range(STEP // BLOCK):
                body(b * STEP + part * BLOCK)
            return carry

        lax.fori_loop(first // STEP, last // STEP, step, 0)

    def each_section(body):
        def step(i, carry):
            body(1 - i)
            return carry

        lax.fori_loop(0, 2, step, 0)

    def unfold(from_ref, to_ref):
        def body(i, carry):
            section, part = 1 - i // 2, i % 2
            for t in range(lines // SUB):
                rows = from_ref[section, part, pl.ds(t * SUB, SUB), :]
                to_ref[section, part, pl.ds(t * SUB, SUB)] = rows.reshape(SUB, SUB, LANES)
            return carry

        lax.fori_loop(0, 4, body, 0)

    def take_adjoint():
        load_adjoint.wait()
        push_pair(0, adjoint_hbm, adjoint_in, 1 - core).wait_recv()
        unfold(adjoint_in, adj)

    def take_source():
        load_source.wait()
        push_pair(1, source_hbm, source_in, 1 - core).wait_recv()
        unfold(source_in, wave)

    def filter_y(section, y, adjoint):
        return filtered(
            lambda o: tuple(padded[section, part, block(y + reach + o)] for part in range(3)),
            taps, adjoint,
        )

    def put_padded(section, y, re, im):
        padded[section, 0, block(y + reach)] = re
        padded[section, 1, block(y + reach)] = im
        padded[section, 2, block(y + reach)] = re + im

    def slow_block(section, y):
        if whole_lines:
            return slow[section, block(y)]
        rows = slow[section, pl.ds(y * per_line, BLOCK * per_line)]
        return rows.reshape(BLOCK, SUB, LANES)

    def add_grad(section, y, term):
        if whole_lines:
            grad[section, block(y)] += term
        else:
            grad[section, pl.ds(y * per_line, BLOCK * per_line)] += term.reshape(
                BLOCK * per_line, SUB // per_line, LANES
            )

    def phases(section, first=0, last=lines):
        def body(y):
            s, co = sin_cos(w * slow_block(section, y))
            sine[section, block(y)] = s
            cosine[section, block(y)] = co

        each_block(first, last, body)

    def forward(section, finish):
        def along_x(y):
            re, im = wave[section, 0, block(y)], wave[section, 1, block(y)]
            put_padded(section, y, *filter_x(re, im, taps, False))

        def along_y(y):
            finish(section, y, *filter_y(section, y, False))

        each_block(0, lines, along_x)
        each_block(0, lines, along_y)

    def turned(section, y, re, im):
        co, s = cosine[section, block(y)], sine[section, block(y)]
        return w * (co * re - s * im), w * (s * re + co * im)

    def hop(chunk):
        rows = pl.ds(chunk * CHUNK, CHUNK)
        return pltpu.make_async_remote_copy(
            src_ref=leaving.at[rows], dst_ref=arrived.at[rows],
            send_sem=mu_send.at[chunk], recv_sem=mu_recv.at[chunk],
            device_id={"depth": lax.max(d - 2, 0)}, device_id_type=MESH,
        )

    def chain(before, use, taken, x_first):
        lag = -(-reach // CHUNK)

        def take(section, chunk):
            if section == 1:
                @pl.when(from_below)
                def _():
                    hop(chunk).wait_recv()

            before(section, chunk)
            first, last = chunk * CHUNK, (chunk + 1) * CHUNK
            incoming = arrived if section == 1 else carried

            def mu(y):
                return (
                    adj[section, 0, block(y)] + incoming[block(y), 0],
                    adj[section, 1, block(y)] + incoming[block(y), 1],
                )

            def body(y):
                mu_re, mu_im = mu(y)
                co, s = cosine[section, block(y)], sine[section, block(y)]
                re, im = co * mu_re + s * mu_im, co * mu_im - s * mu_re
                if x_first:
                    re, im = filter_x(re, im, taps, True)
                put_padded(section, y, re, im)

            if section == 1:
                each_block(first, last, body)
            else:
                pl.when(to_above)(lambda: each_block(first, last, body))
            each_block(first, last, lambda y: use(section, y, *mu(y)))

        def give(section, chunk):
            outgoing = carried if section == 1 else leaving

            def body(y):
                re, im = filter_y(section, y, True)
                if not x_first:
                    re, im = filter_x(re, im, taps, True)
                outgoing[block(y), 0] = re
                outgoing[block(y), 1] = im

            each_block(chunk * CHUNK, (chunk + 1) * CHUNK, body)
            if section == 0:
                hop(chunk).start()

        for turn in range(chunks + 2 * lag):
            if turn < chunks:
                take(1, turn)
            if lag <= turn < chunks + lag:
                give(1, turn - lag)
                take(0, turn - lag)
            if turn >= 2 * lag:
                pl.when(to_above)(functools.partial(give, 0, turn - 2 * lag))
            if turn < chunks:
                taken(1, turn)
            if lag <= turn < chunks + lag:
                taken(0, turn - lag)

    def push_grad(to, section, sender):
        return pltpu.make_async_remote_copy(
            src_ref=grad.at[section, piece(to)], dst_ref=gathered.at[sender],
            send_sem=grad_send.at[to * 2 + section], recv_sem=grad_recv.at[sender],
            device_id={"freq": to, "depth": base + section}, device_id_type=MESH,
        )

    def send_grad(section, first, last):
        def step(to, carry):
            @pl.when(to * 2 + section != me)
            def _():
                push_grad(to, section, me).start()

            return carry

        lax.fori_loop(first, last, step, 0)

    early = d >= depths // 2

    @pl.when(early)
    def _():
        take_adjoint()
        lax.fori_loop(1, members, wait_slow, 0)

        @pl.when(from_below)
        def _():
            each_section(phases)

        def before(section, chunk):
            @pl.when(jnp.logical_not(from_below))
            def _():
                phases(section, chunk * CHUNK, (chunk + 1) * CHUNK)

        def keep(section, y, mu_re, mu_im):
            adj[section, 0, block(y)] = mu_re
            adj[section, 1, block(y)] = mu_im

        chain(before, keep, lambda section, chunk: None, False)
        take_source()

        def finish(section, y, re, im):
            re, im = turned(section, y, re, im)
            mu_re, mu_im = adj[section, 0, block(y)], adj[section, 1, block(y)]
            add_grad(section, y, mu_im * re - mu_re * im)

        def last(section):
            forward(section, finish)
            send_grad(section, 0, peers)

        each_section(last)

    @pl.when(jnp.logical_not(early))
    def _():
        take_source()

        def finish(section, y, re, im):
            wave[section, 0, block(y)] = re
            wave[section, 1, block(y)] = im

        each_section(lambda section: forward(section, finish))
        take_adjoint()
        lax.fori_loop(1, members, wait_slow, 0)

        def turn(section):
            phases(section)

            def body(y):
                re, im = turned(section, y, wave[section, 0, block(y)], wave[section, 1, block(y)])
                wave[section, 0, block(y)] = re
                wave[section, 1, block(y)] = im

            each_block(0, lines, body)

        each_section(turn)

        def use(section, y, mu_re, mu_im):
            re, im = wave[section, 0, block(y)], wave[section, 1, block(y)]
            add_grad(section, y, mu_im * re - mu_re * im)

        def taken(section, chunk):
            done = [n * CHUNK * peers // lines for n in (chunk, chunk + 1)]
            send_grad(section, *done)

        chain(lambda section, chunk: None, use, taken, True)

    gathered[me] = grad[core, piece(me // 2)]

    def add(i, total):
        push_grad(me // 2, core, other(i)).wait_recv()
        return total + gathered[other(i)]

    total = lax.fori_loop(1, members, add, gathered[me])
    out_ref[...] = total * (1.0 / count)

    def drain(i, carry):
        push_slow(i, me).wait_send()
        push_grad(other(i) // 2, other(i) % 2, me).wait_send()
        return carry

    lax.fori_loop(1, members, drain, 0)
    push_pair(0, adjoint_hbm, adjoint_in, core).wait_send()
    push_pair(1, source_hbm, source_in, core).wait_send()

    @pl.when(to_above)
    def _():
        def drain_mu(chunk, carry):
            hop(chunk).wait_send()
            return carry

        lax.fori_loop(0, chunks, drain_mu, 0)


def on_device(slowness, freq_index, taps, source_top, adjoint_source):
    lanes, _, _, lines, cells = source_top.shape
    peers, depths = lax.axis_size("freq"), lax.axis_size("depth")
    count, _, width = taps.shape
    reach = width // 2
    assert lanes == 2 and depths % 2 == 0 and cells == SUB * LANES and slowness.shape[0] == 1
    rows = slowness.shape[1] // LANES
    whole_lines = rows % SUB == 0
    piece = (rows // SUB, SUB, LANES) if whole_lines else (1, rows, LANES)
    pieces = (piece[0] * peers,) + piece[1:]
    line = (SUB, LANES)
    f32 = jnp.float32
    vmem = pl.BlockSpec(memory_space=pltpu.VMEM)
    hbm = pl.BlockSpec(memory_space=pltpu.HBM)
    dma = pltpu.SemaphoreType.DMA
    chunks = lines // CHUNK
    out = pl.pallas_call(
        functools.partial(
            kernel, peers, depths, lines, reach, count, piece[0], whole_lines
        ),
        out_shape=jax.ShapeDtypeStruct(piece, f32),
        in_specs=[hbm] * 5,
        out_specs=vmem,
        scratch_shapes=[
            pltpu.VMEM(piece, f32),
            pltpu.SMEM((lanes,), jnp.int32),
            pltpu.SMEM((width, 2, count), f32),
            pltpu.VMEM((2, 2, lines, cells), f32),
            pltpu.VMEM((2, 2, lines, cells), f32),
            pltpu.VMEM((2, 2, lines) + line, f32),
            pltpu.VMEM((2, 2, lines) + line, f32),
            pltpu.VMEM((2, 3, lines + 2 * reach) + line, f32),
            pltpu.VMEM((2,) + pieces, f32),
            pltpu.VMEM((2, lines) + line, f32),
            pltpu.VMEM((2, lines) + line, f32),
            pltpu.VMEM((lines, 2) + line, f32),
            pltpu.VMEM((lines, 2) + line, f32),
            pltpu.VMEM((lines, 2) + line, f32),
            pltpu.VMEM((2,) + pieces, f32),
            pltpu.VMEM((2 * peers,) + piece, f32),
            dma((5,)),
            dma((2,)),
            dma((2,)),
            dma((2 * peers,)),
            dma((2 * peers,)),
            dma((chunks,)),
            dma((chunks,)),
            dma((2 * peers,)),
            dma((2 * peers,)),
        ],
        compiler_params=pltpu.CompilerParams(
            collective_id=0, has_side_effects=True, vmem_limit_bytes=56 * 1024 * 1024
        ),
    )(
        slowness.reshape(piece),
        freq_index,
        taps.transpose(2, 1, 0),
        source_top.reshape(lanes, 2, lines, cells),
        adjoint_source.reshape(lanes, 2, lines, cells),
    )
    return out.reshape(slowness.shape)


def solution(mesh):
    in_specs = (
        P("depth", "freq"),
        P("freq"),
        P(),
        P("freq", "depth", None, None, None),
        P("freq", "depth", None, None, None),
    )
    out_specs = P("depth", "freq")
    return jax.shard_map(
        on_device, mesh=mesh, in_specs=in_specs, out_specs=out_specs, check_vma=False
    )
```

time: 25.1 us -> 26.5 us (1.056)
  Pallas kernels: 23.5 us -> 24.8 us
    pallas_call x1, Pallas kernels: 23.5 us -> 24.8 us  [on_device(): pl.pallas_call(functools.partial(kernel, peers, depths, lines, reach, cou...]
where the time goes in v5:
time: 26.5 us; the launch traced here: 26.2 us
  Pallas kernels  24.8 us (94%)
  local copies, waits for them, and re-layouts  1.31 us (5%)
    pallas_call x1, Pallas kernels, on_device(): pl.pallas_call(functools.partial(kernel, peers, depths, lines, reach, cou...  24.8 us
    unnamed x1, local copies, waits for them, and re-layouts  1.31 us

profile of v5, /device:TPU:0, one launch (start us, length us, event | category | flops | bytes accessed | tf_op | source)
XLA Modules:
  0.0 26.2 jit_solution(13464857149961682435)
XLA Ops:
  0.0 24.8 %shard_map.55 = f32[3,8,128]{2,1,0:T(8,128)} custom-call(f32[3,8,128]{2,1,0:T(8,128)} %bitcast.8, s32[2]{0:T(128)} %index_hbm.1, f32[11,2,16]{2,1,0:T(2,128)} %bitcast.9, f32[2,2,24,1024]{3,2,1,0:T(8,128)} %bitcast.5, f32[2,2,24,1024]{3,2,1,0:T(8,128)} %bitcast.6), custom_call_target="tpu_custom_call" | custom-call | tf_op jit(solution)/shard_map/pallas_call | solution.py:449
  24.9 1.3 %copy.7 = f32[1,3072]{1,0:T(1,128)} copy(f32[1,3072]{1,0:T(1,128)} %bitcast.7) | data formatting | bytes 24576

commit v6 on v4

--- a/solution.py
+++ b/solution.py
@@ -13,7 +13,7 @@
 SUB = 8
 BLOCK = 4
 STEP = 8
-CHUNK = 4
+CHUNK = 8
 
 PI_HIGH = 3.140625
 PI_LOW = math.pi - PI_HIGH
@@ -137,6 +137,10 @@
         push_slow(i, peer(i)).wait_recv()
         return carry
 
+    def drain_slow(i, carry):
+        push_slow(i, me).wait_send()
+        return carry
+
     def tap_list(f):
         row = index_ref[f]
         return [(taps_ref[k, 0, row], taps_ref[k, 1, row]) for k in range(2 * reach + 1)]
@@ -328,6 +332,7 @@
                 phases(f, chunk * CHUNK, (chunk + 1) * CHUNK)
 
         each_lane(lambda f: chain(f, before, keep, lambda f, chunk: None, False))
+        lax.fori_loop(1, peers, drain_slow, 0)
         load_source.wait()
         unfold(source_in, wave)
 
@@ -363,6 +368,7 @@
             each_block(0, lines, body)
 
         each_lane(turn)
+        lax.fori_loop(1, peers, drain_slow, 0)
 
         def use(f, y, mu_re, mu_im):
             add_grad(y, mu_im * wave[f, 0, block(y)] - mu_re * wave[f, 1, block(y)])
@@ -385,7 +391,6 @@
     out_ref[...] = total * (1.0 / count)
 
     def drain(i, carry):
-        push_slow(i, me).wait_send()
         push_grad(peer(i), me).wait_send()
         return carry
 

time: 25.1 us -> 25.6 us (1.020)
  Pallas kernels: 23.5 us -> 24 us
    pallas_call x1, Pallas kernels: 23.5 us -> 24 us  [on_device(): pl.pallas_call(functools.partial(kernel, peers, depths, lanes, lines, rea...]
where the time goes in v6:
time: 25.6 us; the launch traced here: 25.3 us
  Pallas kernels  24 us (94%)
  local copies, waits for them, and re-layouts  1.31 us (5%)
    pallas_call x1, Pallas kernels, on_device(): pl.pallas_call(functools.partial(kernel, peers, depths, lanes, lines, rea...  24 us
    unnamed x1, local copies, waits for them, and re-layouts  1.31 us

profile of v6, /device:TPU:0, one launch (start us, length us, event | category | flops | bytes accessed | tf_op | source)
XLA Modules:
  0.0 25.3 jit_solution(18269007836300012829)
XLA Ops:
  0.0 24.0 %shard_map.55 = f32[3,8,128]{2,1,0:T(8,128)} custom-call(f32[3,8,128]{2,1,0:T(8,128)} %bitcast.8, s32[2]{0:T(128)} %index_hbm.1, f32[11,2,16]{2,1,0:T(2,128)} %bitcast.9, f32[2,2,24,1024]{3,2,1,0:T(8,128)} %bitcast.5, f32[2,2,24,1024]{3,2,1,0:T(8,128)} %bitcast.6), custom_call_target="tpu_custom_call" | custom-call | tf_op jit(solution)/shard_map/pallas_call | solution.py:424
  24.0 1.3 %copy.7 = f32[1,3072]{1,0:T(1,128)} copy(f32[1,3072]{1,0:T(1,128)} %bitcast.7) | data formatting | bytes 24576

commit v7 on v6

--- a/solution.py
+++ b/solution.py
@@ -13,7 +13,7 @@
 SUB = 8
 BLOCK = 4
 STEP = 8
-CHUNK = 8
+CHUNK = 4
 
 PI_HIGH = 3.140625
 PI_LOW = math.pi - PI_HIGH
@@ -241,57 +241,56 @@
             device_id={"depth": lax.max(d - 1, 0)}, device_id_type=MESH,
         )
 
-    def chain(f, before, use, taken, x_first):
+    def chain(f, before, use, taken):
         taps = tap_list(f)
         lag = -(-reach // CHUNK)
 
+        def mu(y):
+            return adj[f, 0, block(y)] + arrived[f, block(y), 0], adj[f, 1, block(y)] + arrived[f, block(y), 1]
+
+        def use_chunk(chunk):
+            each_block(chunk * CHUNK, (chunk + 1) * CHUNK, lambda y: use(f, y, *mu(y)))
+
         def take(chunk):
+            def body(y):
+                mu_re, mu_im = mu(y)
+                co, s = cosine[f, block(y)], sine[f, block(y)]
+                re, im = co * mu_re + s * mu_im, co * mu_im - s * mu_re
+                put_padded(y, *filter_x(re, im, taps, True))
+
+            each_block(chunk * CHUNK, (chunk + 1) * CHUNK, body)
+
+        def give(chunk):
+            def body(y):
+                re, im = filter_y(y, taps, True)
+                leaving[f, block(y), 0] = re
+                leaving[f, block(y), 1] = im
+
+            each_block(chunk * CHUNK, (chunk + 1) * CHUNK, body)
+            hop(f, chunk).start()
+
+        for chunk in range(chunks):
             @pl.when(d < depths - 1)
             def _():
                 hop(f, chunk).wait_recv()
 
             before(f, chunk)
-            first, last = chunk * CHUNK, (chunk + 1) * CHUNK
-
-            def mu(y):
-                return adj[f, 0, block(y)] + arrived[f, block(y), 0], adj[f, 1, block(y)] + arrived[f, block(y), 1]
 
             @pl.when(d > 0)
             def _():
-                def body(y):
-                    mu_re, mu_im = mu(y)
-                    co, s = cosine[f, block(y)], sine[f, block(y)]
-                    re, im = co * mu_re + s * mu_im, co * mu_im - s * mu_re
-                    if x_first:
-                        re, im = filter_x(re, im, taps, True)
-                    put_padded(y, re, im)
-
-                each_block(first, last, body)
-
-            each_block(first, last, lambda y: use(f, y, *mu(y)))
-
-        def give(chunk):
-            @pl.when(d > 0)
-            def _():
-                def body(y):
-                    re, im = filter_y(y, taps, True)
-                    if not x_first:
-                        re, im = filter_x(re, im, taps, True)
-                    leaving[f, block(y), 0] = re
-                    leaving[f, block(y), 1] = im
-
-                each_block(chunk * CHUNK, (chunk + 1) * CHUNK, body)
-                hop(f, chunk).start()
-
-        for chunk in range(chunks):
-            take(chunk)
-            if chunk >= lag:
-                give(chunk - lag)
-            if chunk < chunks - 1:
-                taken(f, chunk)
-        for chunk in range(chunks - lag, chunks):
-            give(chunk)
-        taken(f, chunks - 1)
+                take(chunk)
+                if chunk >= lag:
+                    give(chunk - lag)
+                if chunk == chunks - 1:
+                    for last in range(chunks - lag, chunks):
+                        give(last)
+                use_chunk(chunk)
+
+            @pl.when(d == 0)
+            def _():
+                use_chunk(chunk)
+
+            taken(f, chunk)
 
     def push_grad(to, sender):
         return pltpu.make_async_remote_copy(
@@ -331,7 +330,7 @@
             def _():
                 phases(f, chunk * CHUNK, (chunk + 1) * CHUNK)
 
-        each_lane(lambda f: chain(f, before, keep, lambda f, chunk: None, False))
+        each_lane(lambda f: chain(f, before, keep, lambda f, chunk: None))
         lax.fori_loop(1, peers, drain_slow, 0)
         load_source.wait()
         unfold(source_in, wave)
@@ -379,7 +378,7 @@
                 done = [n * CHUNK * peers // lines for n in (chunk, chunk + 1)]
                 send_grad(*done)
 
-        each_lane(lambda f: chain(f, lambda f, chunk: None, use, taken, True))
+        each_lane(lambda f: chain(f, lambda f, chunk: None, use, taken))
 
     gathered[me] = grad[piece(me)]
 

time: 25.6 us -> 25.3 us (0.988)
  Pallas kernels: 24 us -> 23.7 us
    pallas_call x1, Pallas kernels: 24 us -> 23.7 us  [on_device(): pl.pallas_call(functools.partial(kernel, peers, depths, lanes, lines, rea...]
where the time goes in v7:
time: 25.3 us; the launch traced here: 25 us
  Pallas kernels  23.7 us (94%)
  local copies, waits for them, and re-layouts  1.31 us (5%)
    pallas_call x1, Pallas kernels, on_device(): pl.pallas_call(functools.partial(kernel, peers, depths, lanes, lines, rea...  23.7 us
    unnamed x1, local copies, waits for them, and re-layouts  1.31 us

profile of v7, /device:TPU:0, one launch (start us, length us, event | category | flops | bytes accessed | tf_op | source)
XLA Modules:
  0.0 25.0 jit_solution(16820215494382440301)
XLA Ops:
  0.0 23.7 %shard_map.55 = f32[3,8,128]{2,1,0:T(8,128)} custom-call(f32[3,8,128]{2,1,0:T(8,128)} %bitcast.8, s32[2]{0:T(128)} %index_hbm.1, f32[11,2,16]{2,1,0:T(2,128)} %bitcast.9, f32[2,2,24,1024]{3,2,1,0:T(8,128)} %bitcast.5, f32[2,2,24,1024]{3,2,1,0:T(8,128)} %bitcast.6), custom_call_target="tpu_custom_call" | custom-call | tf_op jit(solution)/shard_map/pallas_call | solution.py:423
  23.7 1.3 %copy.7 = f32[1,3072]{1,0:T(1,128)} copy(f32[1,3072]{1,0:T(1,128)} %bitcast.7) | data formatting | bytes 24576

commit v8 on v7

--- a/solution.py
+++ b/solution.py
@@ -33,16 +33,20 @@
     return sign * rest * odd, sign * even
 
 
-def shifted(value, reach):
+def shifter(value):
     lane = lax.broadcasted_iota(jnp.int32, value.shape, 2)
     row = lax.broadcasted_iota(jnp.int32, value.shape, 1)
     after = jnp.where(row < SUB - 1, pltpu.roll(value, SUB - 1, 1), 0.0)
     before = jnp.where(row > 0, pltpu.roll(value, 1, 1), 0.0)
-    out = {0: value}
-    for o in range(1, reach + 1):
-        out[o] = pltpu.roll(jnp.where(lane >= o, value, after), LANES - o, 2)
-        out[-o] = pltpu.roll(jnp.where(lane < LANES - o, value, before), o, 2)
-    return out
+
+    def shifted(o):
+        if o > 0:
+            return pltpu.roll(jnp.where(lane >= o, value, after), LANES - o, 2)
+        if o < 0:
+            return pltpu.roll(jnp.where(lane < LANES + o, value, before), -o, 2)
+        return value
+
+    return shifted
 
 
 def filtered(at, taps, adjoint):
@@ -60,9 +64,13 @@
 
 
 def filter_x(re, im, taps, adjoint):
-    reach = len(taps) // 2
-    all_re, all_im = shifted(re, reach), shifted(im, reach)
-    return filtered(lambda o: (all_re[o], all_im[o], all_re[o] + all_im[o]), taps, adjoint)
+    shift_re, shift_im = shifter(re), shifter(im)
+
+    def at(o):
+        u_re, u_im = shift_re(o), shift_im(o)
+        return u_re, u_im, u_re + u_im
+
+    return filtered(at, taps, adjoint)
 
 
 def kernel(

time: 25.3 us -> 25.3 us (level)
  no operation moved by 1% of the time
where the time goes in v8:
time: 25.3 us; the launch traced here: 25 us
  Pallas kernels  23.6 us (93%)
  local copies, waits for them, and re-layouts  1.31 us (5%)
    pallas_call x1, Pallas kernels, on_device(): pl.pallas_call(functools.partial(kernel, peers, depths, lanes, lines, rea...  23.6 us
    unnamed x1, local copies, waits for them, and re-layouts  1.31 us

profile of v8, /device:TPU:0, one launch (start us, length us, event | category | flops | bytes accessed | tf_op | source)
XLA Modules:
  0.0 25.0 jit_solution(15684724447439647361)
XLA Ops:
  0.0 23.6 %shard_map.55 = f32[3,8,128]{2,1,0:T(8,128)} custom-call(f32[3,8,128]{2,1,0:T(8,128)} %bitcast.8, s32[2]{0:T(128)} %index_hbm.1, f32[11,2,16]{2,1,0:T(2,128)} %bitcast.9, f32[2,2,24,1024]{3,2,1,0:T(8,128)} %bitcast.5, f32[2,2,24,1024]{3,2,1,0:T(8,128)} %bitcast.6), custom_call_target="tpu_custom_call" | custom-call | tf_op jit(solution)/shard_map/pallas_call | solution.py:431
  23.7 1.3 %copy.7 = f32[1,3072]{1,0:T(1,128)} copy(f32[1,3072]{1,0:T(1,128)} %bitcast.7) | data formatting | bytes 24576
